TPU v7x, 32 devices: a whole 2x2x4 slice. The times are simulated.
32 devices in a mesh: blk: 8 (over z, x), cols: 4 (over y, core).
Axes of the slice: x: 2, y: 2, z: 4, core: 2. Of those that a mesh axis runs over, the one named last changes fastest.
Arguments:
- focusing_plus: float32 [9728, 16, 512], P(('cols', 'blk')), may hold values from -6 to 6
- direct_field: float32 [9728, 16, 512], P(('cols', 'blk')), may hold values from -4 to 4
- reflectivity: float32 [2, 2, 9728, 9728], P(None, None, 'blk', 'cols'), may hold values from -0.0625 to 0.0625
- frequency_bins: int32 [2], replicated, may hold values from 64 to 247
- focal_onsets: int32 [16], replicated, may hold values from 32 to 191
- line_offsets: int32 [128], replicated, may hold values from 0 to 63
Outputs:
- focusing_update: float32 [9728, 16, 512], P(('cols', 'blk'))
All inputs are finite; a program needn't handle non-finite values.
Results may differ from a plain program's by a relative error of at most 0.000092.
Values sent between devices are 32-bit elements; how exact they have to be, the bound alone decides.
A program may use at most 128 MiB of HBM per device.

v0:
```python
import math

import jax
import jax.numpy as jnp
from jax import lax
from jax.sharding import PartitionSpec as P

LINE = 76


highest = lax.Precision.HIGHEST


def wave_tables(frequency_bins, samples):
    times = jnp.arange(samples, dtype=jnp.int32)
    phases = frequency_bins[:, None] * times[None, :] % samples
    angles = phases.astype(jnp.float32) * (2.0 * math.pi / samples)
    inverse = jnp.stack([jnp.cos(angles), -jnp.sin(angles)], axis=1).reshape(-1, samples)
    forward = inverse / math.sqrt(samples)
    return (forward, inverse)


def to_spectrum(signal, forward):
    positions, focal, samples = signal.shape
    flat = signal.reshape(positions * focal, samples)
    result = lax.dot_general(
        forward,
        flat,
        (((1,), (1,)), ((), ())),
        precision=highest,
        preferred_element_type=jnp.float32,
    )
    return result.reshape(-1, 2, positions, focal)


def to_signal(spectrum, inverse):
    waves, halves, positions, focal = spectrum.shape
    flat = spectrum.reshape(waves * halves, positions * focal)
    result = lax.dot_general(
        flat,
        inverse,
        (((0,), (0,)), ((), ())),
        precision=highest,
        preferred_element_type=jnp.float32,
    )
    return result.reshape(positions, focal, -1)


def apply_window(signal, first_row, focal_onsets, line_offsets, line_length):
    positions, focal, samples = signal.shape
    lines = lax.dynamic_slice_in_dim(
        line_offsets, first_row // line_length, positions // line_length
    )
    per_row = jnp.repeat(lines, line_length)
    onsets = focal_onsets[None, :] + per_row[:, None]
    times = jnp.arange(samples, dtype=jnp.int32)
    window = (times[None, None, :] < onsets[:, :, None]) | (
        times[None, None, :] >= samples - onsets[:, :, None]
    )
    return jnp.where(window, signal, jnp.zeros_like(signal))


def kernel_apply(kernel, spectrum):
    parts = jnp.einsum("wprs,wqsf->wpqrf", kernel, spectrum, precision=highest)
    real = parts[:, 0, 0] - parts[:, 1, 1]
    imag = parts[:, 0, 1] + parts[:, 1, 0]
    return jnp.stack([real, imag], axis=1)


def adjoint_rows(kernel, spectrum):
    parts = jnp.einsum("wprs,wqrf->swpqf", kernel, spectrum, precision=highest)
    real = parts[:, :, 0, 0] + parts[:, :, 1, 1]
    imag = parts[:, :, 0, 1] - parts[:, :, 1, 0]
    stacked = jnp.stack([real, imag], axis=2)
    return stacked.reshape(stacked.shape[0], -1)


def local(focusing_plus, direct_field, reflectivity, frequency_bins, focal_onsets, line_offsets):
    samples = focusing_plus.shape[2]
    focal = focusing_plus.shape[1]
    waves = reflectivity.shape[0]
    block_rows = reflectivity.shape[2]
    group_columns = reflectivity.shape[3]
    own_sources = focusing_plus.shape[0]
    forward, inverse = wave_tables(frequency_bins, samples)
    own_spectrum = to_spectrum(focusing_plus, forward)
    gathered = lax.all_gather(own_spectrum, "blk", axis=2, tiled=True)
    partial_value = kernel_apply(reflectivity, gathered)
    block_index = lax.axis_index("blk")
    group_index = lax.axis_index("cols")
    share = lax.psum_scatter(partial_value, "cols", scatter_dimension=2, tiled=True)
    share_rows = share.shape[2]
    first_share = block_index * block_rows + group_index * share_rows
    minus_signal = apply_window(
        to_signal(share, inverse), first_share, focal_onsets, line_offsets, LINE
    )
    minus_rows = lax.all_gather(to_spectrum(minus_signal, forward), "cols", axis=2, tiled=True)
    summed = lax.psum_scatter(
        adjoint_rows(reflectivity, minus_rows), "blk", scatter_dimension=0, tiled=True
    )
    update = summed.reshape(own_sources, waves, 2, focal).transpose(1, 2, 0, 3)
    first_source = group_index * group_columns + block_index * own_sources
    correction = apply_window(
        to_signal(update, inverse), first_source, focal_onsets, line_offsets, LINE
    )
    return direct_field - correction


def solution(mesh):
    return jax.shard_map(
        local,
        mesh=mesh,
        in_specs=(
            P(("cols", "blk"), None, None),
            P(("cols", "blk"), None, None),
            P(None, None, "blk", "cols"),
            P(),
            P(),
            P(),
        ),
        out_specs=P(("cols", "blk"), None, None),
        check_vma=False,
    )
```

profile of v0, /device:TPU:0, one launch (start us, length us, event | category | flops | bytes accessed | tf_op | source)
XLA Modules:
  0.0 403.1 jit_solution(17016666350454153220)
XLA Ops:
  6.5 0.0 reduce-scatter.7.cloned.1.call-start
  6.5 0.9 fusion.40
  7.4 18.0 %fusion.6 = f32[2,2,304,16]{2,1,3,0:T(2,128)S(1)} fusion(f32[304,16,512]{2,1,0:T(8,128)} %param.6, f32[2,1,512]{2,1,0:T(1,128)S(1)} %get-tuple-element.14, f32[2,1,512]{2,1,0:T(1,128)S(1)} %get-tuple-element.13), kind=kOutput, calls=%fused_computation.6 | convolution fusion | flops 119541760 | bytes 10047488 | tf_op jit(solution)/shard_map/dot_general | solution.py:26
  25.4 0.4 copy.20
  25.8 99.3 %all_gather.6 = f32[2,2,2432,16]{3,1,0,2:T(2,128)S(1)} all-gather(f32[2,2,304,16]{3,1,0,2:T(2,128)S(1)} %copy.20), channel_id=1, replica_groups=mesh['blk'=8,'cols'=4] {'blk'}, dimensions={2}, use_global_device_ids=true | all-gather | bytes 700416 | tf_op jit(solution)/shard_map/all_gather | solution.py:87
  125.1 0.0 copy-start
  125.1 0.0 copy-start.1
  125.1 82.4 %fusion.18 = f32[2,2,2,1216,16]{3,4,1,2,0:T(8,128)S(1)} fusion(f32[2,2,1216,2432]{3,2,1,0:T(8,128)} %param.8, f32[2,2,2432,16,1]{3,1,0,2,4:T(2,128)S(1)} %bitcast.78), kind=kOutput, calls=%fused_computation.21 | convolution fusion | flops 4542431232 | bytes 48562176 | tf_op jit(solution)/shard_map/wprs,wqsf->wpqrf/dot_general | solution.py:64
  207.6 2.2 copy.42
  209.8 2.7 reshape.322
  212.5 0.0 reduce-scatter.7.cloned.1.call-update
  212.5 0.0 reduce-scatter.9.cloned.1.call-start
  212.7 0.0 copy-done
  212.7 0.1 fusion.43
  212.7 0.1 broadcast_in_dim.5
  212.8 0.1 add.112
  212.9 0.1 broadcast_in_dim.4
  213.0 0.1 add.106
  213.1 0.0 copy-done.1
  213.1 0.1 broadcast_add_fusion
  213.3 21.6 %reduce-scatter.7.cloned.1.call-done = f32[304,64]{1,0:T(8,128)} async-done(((f32[1216,64]{1,0:T(8,128)}), f32[304,64]{1,0:T(8,128)}) %reduce-scatter.7.cloned.1.call-update) | async-done | bytes 77840
  234.8 1.4 reshape.323
  236.3 0.3 reshape.309
  236.6 0.2 dot_general.29
  236.8 11.0 %fusion.12 = f32[304,16,512]{2,1,0:T(8,128)S(1)} fusion(s32[304,16]{1,0:T(8,128)S(1)} %get-tuple-element.6, s32[304,16]{1,0:T(8,128)S(1)} %get-tuple-element.5, f32[4,512,1]{1,0,2:T(4,128)S(1)} %reshape.318, f32[304,16,4]{1,0,2:T(8,128)S(1)} %dot_general.29), kind=kOutput, calls=%fused_computation.17 | convolution fusion | flops 129499136 | bytes 10086400 | tf_op jit(solution)/shard_map/dot_general | solution.py:39
  247.8 14.2 %fusion.4 = f32[2,2,304,16]{2,1,3,0:T(2,128)S(1)} fusion(f32[304,16,512]{2,1,0:T(8,128)S(1)} %fusion.12, f32[2,1,512]{2,1,0:T(1,128)S(1)} %get-tuple-element.14, f32[2,1,512]{2,1,0:T(1,128)S(1)} %get-tuple-element.13), kind=kOutput, calls=%fused_computation.4 | convolution fusion | flops 119541760 | bytes 10047488 | tf_op jit(solution)/shard_map/dot_general | solution.py:26
  262.0 0.4 copy.27
  262.4 17.5 %all_gather.7 = f32[2,2,1216,16]{3,1,0,2:T(2,128)S(1)} all-gather(f32[2,2,304,16]{3,1,0,2:T(2,128)S(1)} %copy.27), channel_id=1, replica_groups=mesh['blk'=8,'cols'=4] {'cols'}, dimensions={2}, use_global_device_ids=true | all-gather | bytes 389120 | tf_op jit(solution)/shard_map/all_gather | solution.py:97
  279.9 33.0 %fusion.14 = f32[2432,2,2,2,16]{0,4,2,3,1:T(8,128)S(1)} fusion(f32[2,2,1216,2432]{3,2,1,0:T(8,128)} %param.8, f32[2,2,1216,16,1]{3,1,0,2,4:T(2,128)S(1)} %bitcast.79), kind=kOutput, calls=%fused_computation.19 | convolution fusion | flops 4542431232 | bytes 48873472 | tf_op jit(solution)/shard_map/wprs,wqrf->swpqf/dot_general | solution.py:71
  313.0 1.4 copy.44
  314.4 0.0 reduce-scatter.9.cloned.1.call-update
  314.5 65.3 %reduce-scatter.9.cloned.1.call-done = f32[304,64]{1,0:T(8,128)} async-done(((f32[2432,64]{1,0:T(8,128)}), f32[304,64]{1,0:T(8,128)}) %reduce-scatter.9.cloned.1.call-update) | async-done | bytes 77840
  379.8 1.0 copy.45
  380.8 0.2 copy.32
  381.0 0.3 reshape.313
  381.3 0.2 dot_general.34
  381.6 14.2 %select_subtract_fusion = f32[304,16,512]{2,1,0:T(8,128)} fusion(f32[304,16,512]{2,1,0:T(8,128)} %param.7, s32[304,16]{1,0:T(8,128)S(1)} %get-tuple-element.9, s32[304,16]{1,0:T(8,128)S(1)} %get-tuple-element.10, f32[4,512,1]{1,0,2:T(4,128)S(1)} %reshape.318, f32[304,16,4]{1,0,2:T(8,128)S(1)} %dot_general.34), kind=kOutput, calls=%fused_computation.10 | convolution fusion | flops 131989504 | bytes 20047872 | tf_op jit(solution)/shard_map/dot_general | solution.py:39
  (10 shorter events, 0.3 us)
Async XLA Ops:
  6.5 228.3 %reduce-scatter.7.cloned.1.call-start = ((), (), s32[]{:S(2)}) async-start(), calls=%async_computation.2 | async-start | bytes 778240
  125.1 87.5 %copy-start = (s32[128]{0:T(128)S(1)}, s32[128]{0:T(128)}, u32[]{:S(2)}) copy-start(s32[128]{0:T(128)} %param.11) | copy-start | bytes 1540
  125.1 88.0 %copy-start.1 = (s32[16]{0:T(128)S(1)}, s32[16]{0:T(128)}, u32[]{:S(2)}) copy-start(s32[16]{0:T(128)} %param.10) | copy-start | bytes 196
  212.5 167.2 %reduce-scatter.9.cloned.1.call-start = ((), (), s32[]{:S(2)}) async-start(), calls=%async_computation.3 | async-start | bytes 1400832
Sparse Core Ops, SparseCore 0:
  212.7 22.1 reduce-scatter.6
  314.6 65.1 reduce-scatter.8
where the time goes:
time: 409 us; the launch traced here: 403 us
  matrix products  173 us (42%)
  blocking collectives  117 us (29%)
  waiting for transfers between devices  86.9 us (21%)
  between operations  14.1 us (3%)
  local copies, waits for them, and re-layouts  11.3 us (3%)
    all_gather x1, blocking collectives, local(): gathered = lax.all_gather(own_spectrum, 'blk', axis=2, tiled=True)  99.3 us
    unnamed x4, waiting for transfers between devices  86.9 us
    dot_general x1, matrix products, kernel_apply(): parts = jnp.einsum('wprs,wqsf->wpqrf', kernel, spectrum, precision=highest)  82.4 us
    dot_general x1, matrix products, adjoint_rows(): parts = jnp.einsum('wprs,wqrf->swpqf', kernel, spectrum, precision=highest)  33 us
    dot_general x2, matrix products, to_spectrum(): lax.dot_general(forward, flat, (((1,), (1,)), ((), ())), precision=highes...  32.2 us
    dot_general x2, matrix products, to_signal(): lax.dot_general(flat, inverse, (((0,), (0,)), ((), ())), precision=highes...  25.2 us
    all_gather x1, blocking collectives, local(): lax.all_gather(to_spectrum(minus_signal, forward), 'cols', axis=2, tiled=...  17.5 us
    unnamed x9, local copies, waits for them, and re-layouts  8.75 us
  transfers between devices with their start and end apart: 2, of which 2 were waited for; matrix products, arithmetic and copies ran while one was open for 0% of the time, Pallas kernels for 0%

commit v1 on v0

v1 whole, which is shorter than its diff:
```python
import math

import jax
import jax.numpy as jnp
from jax import lax
from jax.sharding import PartitionSpec as P

LINE = 76


high = lax.Precision.HIGH
highest = lax.Precision.HIGHEST


def wave_tables(frequency_bins, samples):
    times = jnp.arange(samples, dtype=jnp.int32)
    phases = frequency_bins[:, None] * times[None, :] % samples
    angles = phases.astype(jnp.float32) * (2.0 * math.pi / samples)
    inverse = jnp.stack([jnp.cos(angles), -jnp.sin(angles)], axis=1).reshape(-1, samples)
    forward = inverse / math.sqrt(samples)
    return (forward, inverse)


def windows(first_row, positions, focal_onsets, line_offsets, samples):
    lines = lax.dynamic_slice_in_dim(line_offsets, first_row // LINE, positions // LINE)
    onsets = (focal_onsets[:, None] + lines[None, :])[:, :, None]
    times = jnp.arange(samples, dtype=jnp.int32)
    return (times < onsets) | (times >= samples - onsets)


def local(focusing_plus, direct_field, reflectivity, frequency_bins, focal_onsets, line_offsets):
    own, focal, samples = focusing_plus.shape
    waves, _, block_rows, group_columns = reflectivity.shape
    forward, inverse = wave_tables(frequency_bins, samples)
    block_index = lax.axis_index("blk")
    group_index = lax.axis_index("cols")
    rows = 2 * waves * focal

    spectrum = lax.dot_general(
        forward, focusing_plus.reshape(own * focal, samples), (((1,), (1,)), ((), ())),
        precision=high, preferred_element_type=jnp.float32,
    )
    spectrum = spectrum.reshape(-1, own, focal).transpose(0, 2, 1).reshape(rows, own)
    gathered = lax.all_gather(spectrum, "blk", axis=0).transpose(1, 0, 2)
    gathered = gathered.reshape(waves, 2, focal, group_columns)
    real, imag = gathered[:, 0], gathered[:, 1]
    left = jnp.stack(
        [jnp.concatenate([real, imag], 1), jnp.concatenate([-imag, real], 1)], axis=1
    )
    partial_up = jnp.einsum("wpns,wprs->wnr", left, reflectivity, precision=high)
    groups = block_rows // own
    partial_up = partial_up.reshape(rows, groups, own).transpose(1, 0, 2)
    share = lax.psum_scatter(partial_up, "cols", scatter_dimension=0)

    first_share = block_index * block_rows + group_index * own
    window = windows(first_share, own, focal_onsets, line_offsets, samples)
    mix = jnp.einsum(
        "flt,kjt->kjfl", window.astype(jnp.float32), forward[:, None] * inverse[None],
        precision=highest,
    )
    mix = jnp.repeat(mix, LINE, axis=3)
    share = share.reshape(2 * waves, focal, own)
    minus = (mix * share[None]).sum(axis=1).reshape(rows, own)

    minus = lax.all_gather(minus, "cols", axis=0).transpose(1, 0, 2)
    minus = minus.reshape(waves, 2, focal, block_rows)
    real, imag = minus[:, 0], minus[:, 1]
    left = jnp.stack(
        [jnp.concatenate([real, imag], 1), jnp.concatenate([imag, -real], 1)], axis=1
    )
    partial_adj = jnp.einsum("wpnr,wprs->wns", left, reflectivity, precision=high)
    partial_adj = partial_adj.reshape(rows, group_columns // own, own).transpose(1, 0, 2)
    update = lax.psum_scatter(partial_adj, "blk", scatter_dimension=0)

    first_source = group_index * group_columns + block_index * own
    window = windows(first_source, own, focal_onsets, line_offsets, samples)
    window = jnp.repeat(window.transpose(1, 0, 2), LINE, axis=0)
    update = update.reshape(2 * waves, focal, own).transpose(0, 2, 1).reshape(2 * waves, -1)
    correction = lax.dot_general(
        update, inverse, (((0,), (0,)), ((), ())),
        precision=high, preferred_element_type=jnp.float32,
    ).reshape(own, focal, samples)
    return direct_field - jnp.where(window, correction, jnp.zeros_like(correction))


def solution(mesh):
    return jax.shard_map(
        local,
        mesh=mesh,
        in_specs=(
            P(("cols", "blk"), None, None),
            P(("cols", "blk"), None, None),
            P(None, None, "blk", "cols"),
            P(),
            P(),
            P(),
        ),
        out_specs=P(("cols", "blk"), None, None),
        check_vma=False,
    )
```

time: 409 us -> 213 us (0.52); the launches traced: 403 us -> 213 us
  matrix products: 173 us -> 66.7 us
  blocking collectives: 117 us -> 40 us
  local copies, waits for them, and re-layouts: 11.3 us -> 6.76 us
    dot_general x6 -> x5, matrix products: 173 us -> 66.7 us  [the longest x1 24.7 us: local(): jnp.einsum('wpns,wprs->wnr', left, reflectivity, precision=high)]
    unnamed x4 -> x2, waiting for transfers between devices: 86.9 us -> 0.03 us
    reduce_scatter x0 -> x2, waiting for transfers between devices: none -> 83.8 us  [the longest x1 62.8 us: local(): update = lax.psum_scatter(partial_adj, 'blk', scatter_dimension=0)]
    all_gather x2, blocking collectives: 117 us -> 40 us  [the longest x1 33.8 us: local(): gathered = lax.all_gather(spectrum, 'blk', axis=0).transpose(1, 0, 2)]
    unnamed x9 -> x4, local copies, waits for them, and re-layouts: 8.75 us -> 0.01 us
where the time goes in v1:
time: 213 us
  waiting for transfers between devices  83.8 us (39%)
  matrix products  66.7 us (31%)
  blocking collectives  40 us (19%)
  between operations  13.7 us (6%)
  local copies, waits for them, and re-layouts  6.76 us (3%)
    reduce_scatter x1, waiting for transfers between devices, local(): update = lax.psum_scatter(partial_adj, 'blk', scatter_dimension=0)  62.8 us
    all_gather x1, blocking collectives, local(): gathered = lax.all_gather(spectrum, 'blk', axis=0).transpose(1, 0, 2)  33.8 us
    dot_general x1, matrix products, local(): jnp.einsum('wpns,wprs->wnr', left, reflectivity, precision=high)  24.7 us
    reduce_scatter x1, waiting for transfers between devices, local(): share = lax.psum_scatter(partial_up, 'cols', scatter_dimension=0)  21 us
    dot_general x1, matrix products, local(): jnp.einsum('wpnr,wprs->wns', left, reflectivity, precision=high)  19 us
    dot_general x1, matrix products, local(): lax.dot_general(forward, focusing_plus.reshape(own * focal, samples), (((...  13.5 us
    dot_general x1, matrix products, local(): lax.dot_general(update, inverse, (((0,), (0,)), ((), ())), precision=high...  9.1 us
    all_gather x1, blocking collectives, local(): minus = lax.all_gather(minus, 'cols', axis=0).transpose(1, 0, 2)  6.15 us
  transfers between devices with their start and end apart: 2, of which 2 were waited for; matrix products, arithmetic and copies ran while one was open for 0% of the time, Pallas kernels for 0%

profile of v1, /device:TPU:0, one launch (start us, length us, event | category | flops | bytes accessed | tf_op | source)
XLA Modules:
  0.0 212.7 jit_solution(17159484299933473054)
XLA Ops:
  6.5 0.0 reduce-scatter.3.cloned.1.call-start
  6.5 0.9 fusion.27
  7.4 13.5 %fusion.5 = f32[4,16,304]{2,0,1:T(4,128)S(1)} fusion(f32[304,16,512]{2,1,0:T(8,128)} %param.6, f32[4,512]{1,0:T(4,128)S(1)} %reshape.236), kind=kOutput, calls=%fused_computation.8 | convolution fusion | flops 59770880 | bytes 10047488 | tf_op jit(solution)/shard_map/dot_general | solution.py:39
  21.0 33.8 %all_gather.6 = f32[8,64,304]{2,1,0:T(8,128)S(1)} all-gather(f32[1,64,304]{2,1,0:T(8,128)S(1)} %bitcast.75), channel_id=1, replica_groups=mesh['blk'=8,'cols'=4] {'blk'}, dimensions={0}, use_global_device_ids=true | all-gather | bytes 700416 | tf_op jit(solution)/shard_map/all_gather | solution.py:44
  54.8 0.5 copy.69
  55.3 0.3 reshape.237
  55.6 0.1 maximum_bitcast_fusion
  55.7 0.0 copy-start
  55.7 0.0 copy-start.1
  55.8 24.7 %convolution_bitcast_fusion.1 = f32[2,32,1216]{2,1,0:T(8,128)S(1)} fusion(f32[2,2,1216,2432]{3,2,1,0:T(8,128)} %param.8, f32[2,1,32,2432]{3,2,1,0:T(8,128)S(1)} %get-tuple-element.10, f32[2,1,32,2432]{3,2,1,0:T(8,128)S(1)} %get-tuple-element.9), kind=kOutput, calls=%fused_computation.4 | convolution fusion | flops 2271526912 | bytes 48873472 | tf_op jit(solution)/shard_map/wpns,wprs->wnr/dot_general | solution.py:50
  80.4 0.3 reshape.238
  80.7 0.8 copy.99
  81.5 0.0 reduce-scatter.3.cloned.1.call-update
  81.5 0.2 reduce-scatter.5.cloned.1.call-start
  81.8 0.0 copy-done
  81.8 0.1 fusion.32
  81.9 0.0 copy-done.1
  81.9 0.1 broadcast_add_fusion
  82.0 0.4 fusion.15
  82.4 21.0 %reduce-scatter.3.cloned.1.call-done = f32[1,64,304]{2,1,0:T(8,128)} async-done(((f32[4,64,304]{2,1,0:T(8,128)}), f32[1,64,304]{2,1,0:T(8,128)}) %reduce-scatter.3.cloned.1.call-update) | async-done | bytes 77840 | tf_op jit(solution)/shard_map/reduce_scatter | solution.py:53
  103.5 1.0 mul.89
  104.5 0.2 multiply_reduce_fusion
  104.7 0.1 copy.75
  104.8 0.1 all_gather_reshape.7
  104.9 6.1 %all_gather.7 = f32[4,64,304]{2,1,0:T(8,128)S(1)} all-gather(f32[1,64,304]{2,1,0:T(8,128)S(1)} %all_gather_reshape.7), channel_id=1, replica_groups=mesh['blk'=8,'cols'=4] {'cols'}, dimensions={0}, use_global_device_ids=true | all-gather | bytes 389120 | tf_op jit(solution)/shard_map/all_gather | solution.py:65
  111.0 0.3 copy.76
  111.3 0.2 reshape.239
  111.6 19.0 %convolution_bitcast_fusion = f32[2,32,2432]{2,1,0:T(8,128)S(1)} fusion(f32[2,2,1216,2432]{3,2,1,0:T(8,128)} %param.8, f32[2,1,32,1216]{3,2,1,0:T(8,128)S(1)} %get-tuple-element.12, f32[2,1,32,1216]{3,2,1,0:T(8,128)S(1)} %get-tuple-element.11), kind=kOutput, calls=%fused_computation.3 | convolution fusion | flops 2271371264 | bytes 48562176 | tf_op jit(solution)/shard_map/wpnr,wprs->wns/dot_general | solution.py:71
  130.6 0.4 reshape.240
  131.1 1.0 copy.98
  132.1 0.0 reduce-scatter.5.cloned.1.call-update
  132.1 0.1 broadcast_add_fusion.1
  132.2 0.1 fusion.12
  132.3 62.8 %reduce-scatter.5.cloned.1.call-done = f32[1,64,304]{2,1,0:T(8,128)} async-done(((f32[8,64,304]{2,1,0:T(8,128)}), f32[1,64,304]{2,1,0:T(8,128)}) %reduce-scatter.5.cloned.1.call-update) | async-done | bytes 77840 | tf_op jit(solution)/shard_map/reduce_scatter | solution.py:73
  195.1 1.1 copy.81
  196.2 0.3 reshape.241
  196.5 0.2 dot_general.24
  196.8 9.1 %select_subtract_fusion = f32[304,16,512]{2,1,0:T(8,128)} fusion(f32[304,16,512]{2,1,0:T(8,128)} %param.7, pred[4,16,512]{2,1,0:T(8,128)(4,1)S(1)} %fusion.12, f32[4,512,1]{1,0,2:T(4,128)S(1)} %reshape.247, f32[304,16,4]{1,0,2:T(8,128)S(1)} %dot_general.24), kind=kOutput, calls=%fused_computation.2 | convolution fusion | flops 64749568 | bytes 20041728 | tf_op jit(solution)/shard_map/dot_general | solution.py:79
  (12 shorter events, 0.2 us)
Async XLA Ops:
  6.5 96.9 %reduce-scatter.3.cloned.1.call-start = ((), (), s32[]{:S(2)}) async-start(), calls=%async_computation.2 | async-start | bytes 491520 | tf_op jit(solution)/shard_map/reduce_scatter | solution.py:53
  55.7 26.1 %copy-start = (s32[128]{0:T(128)S(1)}, s32[128]{0:T(128)}, u32[]{:S(2)}) copy-start(s32[128]{0:T(128)} %param.11) | copy-start | bytes 1540
  55.7 26.2 %copy-start.1 = (s32[16]{0:T(128)S(1)}, s32[16]{0:T(128)}, u32[]{:S(2)}) copy-start(s32[16]{0:T(128)} %param.10) | copy-start | bytes 196
  81.5 113.6 %reduce-scatter.5.cloned.1.call-start = ((), (), s32[]{:S(2)}) async-start(), calls=%async_computation.3 | async-start | bytes 884736 | tf_op jit(solution)/shard_map/reduce_scatter | solution.py:73
Sparse Core Ops, SparseCore 0:
  81.6 21.7 reduce-scatter.2
  132.3 62.7 reduce-scatter.4

commit v2 on v1

v2 whole, which is shorter than its diff:
```python
import functools
import math

import jax
import jax.numpy as jnp
from jax import lax
from jax.experimental import pallas as pl
from jax.experimental.pallas import tpu as pltpu
from jax.sharding import PartitionSpec as P

LINE = 76
MESH = pl.DeviceIdType.MESH
F32 = jnp.float32
BF16 = jnp.bfloat16


high = lax.Precision.HIGH
highest = lax.Precision.HIGHEST


def wave_tables(frequency_bins, samples):
    times = jnp.arange(samples, dtype=jnp.int32)
    phases = frequency_bins[:, None] * times[None, :] % samples
    angles = phases.astype(jnp.float32) * (2.0 * math.pi / samples)
    inverse = jnp.stack([jnp.cos(angles), -jnp.sin(angles)], axis=1).reshape(-1, samples)
    forward = inverse / math.sqrt(samples)
    return (forward, inverse)


def windows(first_row, positions, focal_onsets, line_offsets, samples):
    lines = lax.dynamic_slice_in_dim(line_offsets, first_row // LINE, positions // LINE)
    onsets = (focal_onsets[:, None] + lines[None, :])[:, :, None]
    times = jnp.arange(samples, dtype=jnp.int32)
    return (times < onsets) | (times >= samples - onsets)


def split(value):
    upper = value.astype(BF16).astype(F32)
    return upper, value - upper


def pieces_of(columns):
    width = 512
    starts = list(range(0, columns, width))
    order = []
    while starts:
        order.append(starts.pop(0))
        if starts:
            order.append(starts.pop())
    return [(start, min(width, columns - start)) for start in order]


def kernel(
    nb, nc, focal, waves, block_rows, group_columns, own, chunk,
    x_hbm, k_hbm, fwd_ref, mix_ref, out_ref,
    xbuf, stage, upper, lower, spec, ag, table, wide, right, up_send, up_recv, mins, left, adj_recv,
    x_sem, k_sem, ag_s, ag_r, up_s, up_r, mi_s, mi_r, ad_s, ad_r,
):
    b = lax.axis_index("blk")
    c = lax.axis_index("cols")
    lines = own // LINE
    lane_tiles = xbuf.shape[1]
    half = 2 * focal
    rows = waves * half
    slots, room = stage.shape[0], xbuf.shape[0]
    chunks = k_hbm.shape[0] // chunk

    def x_copy(line, tile):
        return pltpu.make_async_copy(
            x_hbm.at[pl.ds(line * LINE * focal, LINE * focal), pl.ds(tile * 128, 128)],
            xbuf.at[line % room, tile], x_sem.at[line % room, tile],
        )

    def k_copy(index, slot):
        return pltpu.make_async_copy(
            k_hbm.at[pl.ds(pl.multiple_of(index * chunk, chunk), chunk)],
            stage.at[slot], k_sem.at[slot],
        )

    def to_blk(other):
        return {"blk": other}

    def to_cols(other):
        return {"cols": other}

    for line in range(room):
        for tile in range(lane_tiles):
            x_copy(line, tile).start()
    for slot in range(slots):
        k_copy(slot, slot).start()

    barrier = pltpu.get_barrier_semaphore()
    for d in range(1, nb):
        pl.semaphore_signal(barrier, inc=1, device_id=to_blk(lax.rem(b + d, nb)), device_id_type=MESH)
    for d in range(1, nc):
        pl.semaphore_signal(barrier, inc=1, device_id=to_cols(lax.rem(c + d, nc)), device_id_type=MESH)
    pl.semaphore_wait(barrier, nb + nc - 2)

    fwd = jnp.concatenate(split(fwd_ref[...]), axis=0).astype(BF16)
    for line in range(lines):
        for tile in range(lane_tiles):
            x_copy(line, tile).wait()
        for f in range(focal):
            x = jnp.concatenate(
                [xbuf.at[line % room, tile][pl.ds(f, LINE, stride=focal), :] for tile in range(lane_tiles)], axis=1
            )
            x_upper = x.astype(BF16)
            x_lower = (x - x_upper.astype(F32)).astype(BF16)
            dims = (((1,), (1,)), ((), ()))
            both = lax.dot_general(fwd, x_upper, dims, preferred_element_type=F32)
            both += lax.dot_general(fwd, x_lower, dims, preferred_element_type=F32)
            both = both[: both.shape[0] // 2] + both[both.shape[0] // 2 :]
            for j in range(2 * waves):
                spec[line, j * focal + f : j * focal + f + 1, :] = both[j : j + 1, :]
        if line + room < lines:
            for tile in range(lane_tiles):
                x_copy(line + room, tile).start()
    for line in range(lines):
        ag[b, :, line * LINE : (line + 1) * LINE] = spec[line]

    def ag_copy(d):
        return pltpu.make_async_remote_copy(
            src_ref=ag.at[b], dst_ref=ag.at[b], send_sem=ag_s.at[d], recv_sem=ag_r.at[d],
            device_id=to_blk(lax.rem(b + d, nb)), device_id_type=MESH,
        )

    for d in range(1, nb):
        ag_copy(d).start()

    @pl.loop(0, chunks)
    def _(index):
        slot = lax.rem(index, slots)
        k_copy(index, slot).wait()
        value = stage[slot]
        value_upper = value.astype(BF16)
        place = pl.ds(pl.multiple_of(index * chunk, chunk), chunk)
        upper[place, :] = value_upper
        lower[place, :] = (value - value_upper.astype(F32)).astype(BF16)

        @pl.when(index + slots < chunks)
        def _():
            k_copy(index + slots, slot).start()

    for d in range(1, nb):
        ag_copy(d).wait()
    for other in range(nb):
        wide[:, other * own : (other + 1) * own] = ag[other]

    def operands(value, signs):
        out = []
        for p in range(2):
            stacked = []
            for w in range(waves):
                real = value[w * half : w * half + focal]
                imag = value[w * half + focal : (w + 1) * half]
                pair = [real, imag] if p == 0 else ([-imag, real] if signs else [imag, -real])
                stacked += list(split(jnp.concatenate(pair, axis=0)))
            out.append(jnp.concatenate(stacked, axis=0))
        return out

    for tile in range(group_columns // 128):
        place = slice(tile * 128, (tile + 1) * 128)
        for p, value in enumerate(operands(wide[:, place], True)):
            right[p, place, :] = value.T.astype(BF16)

    def forward_rows(start, count):
        found = []
        for w in range(waves):
            total = None
            for p in range(2):
                place = pl.ds((w * 2 + p) * block_rows + start, count)
                if not isinstance(start, int):
                    place = pl.ds(pl.multiple_of((w * 2 + p) * block_rows + start, 16), count)
                for part in (upper, lower):
                    term = jnp.dot(part[place, :], right[p], preferred_element_type=F32)
                    total = term if total is None else total + term
            turned = total.T
            first = turned[2 * w * half : (2 * w + 1) * half]
            found.append(first + turned[(2 * w + 1) * half : (2 * w + 2) * half])
        return found

    def up_copy(d):
        other = lax.rem(c + d, nc)
        return pltpu.make_async_remote_copy(
            src_ref=up_send.at[other], dst_ref=up_recv.at[d], send_sem=up_s.at[d], recv_sem=up_r.at[d],
            device_id=to_cols(other), device_id_type=MESH,
        )

    if own % 16 == 0:
        for d in list(range(1, nc)) + [0]:
            other = lax.rem(c + d, nc)
            for w, value in enumerate(forward_rows(other * own, own)):
                up_send[other, w * half : (w + 1) * half, :] = value
            if d:
                up_copy(d).start()
    else:
        for w, value in enumerate(forward_rows(0, block_rows)):
            for other in range(nc):
                up_send[other, w * half : (w + 1) * half, :] = value[:, other * own : (other + 1) * own]
        for d in range(1, nc):
            up_copy(d).start()
    share = up_send[c]
    for d in range(1, nc):
        up_copy(d).wait()
        share = share + up_recv[d]

    for k in range(2 * waves):
        total = None
        for j in range(2 * waves):
            at = (k * 2 * waves + j) * focal
            term = mix_ref[at : at + focal, :] * share[j * focal : (j + 1) * focal]
            total = term if total is None else total + term
        mins[c, k * focal : (k + 1) * focal, :] = total

    def mi_copy(d):
        return pltpu.make_async_remote_copy(
            src_ref=mins.at[c], dst_ref=mins.at[c], send_sem=mi_s.at[d], recv_sem=mi_r.at[d],
            device_id=to_cols(lax.rem(c + d, nc)), device_id_type=MESH,
        )

    for d in range(1, nc):
        mi_copy(d).start()
    for d in range(1, nc):
        mi_copy(d).wait()
    for other in range(nc):
        table[:, other * own : (other + 1) * own] = mins[other]
    for p, value in enumerate(operands(table[...], False)):
        left[p] = value.astype(BF16)

    def ad_copy(other):
        d = lax.rem(other - b + nb, nb)
        return pltpu.make_async_remote_copy(
            src_ref=ag.at[other], dst_ref=adj_recv.at[d], send_sem=ad_s.at[d], recv_sem=ad_r.at[d],
            device_id=to_blk(other), device_id_type=MESH,
        )

    done = [False] * group_columns
    sent = set()
    for start, width in pieces_of(group_columns):
        place = slice(start, start + width)
        for w in range(waves):
            total = None
            for p in range(2):
                lhs = left[p, 2 * w * half : (2 * w + 2) * half, :]
                span = slice((w * 2 + p) * block_rows, (w * 2 + p + 1) * block_rows)
                for part in (upper, lower):
                    term = jnp.dot(lhs, part[span, place], preferred_element_type=F32)
                    total = term if total is None else total + term
            wide[w * half : (w + 1) * half, place] = total[:half] + total[half:]
        done[start : start + width] = [True] * width
        for other in range(nb):
            if other not in sent and all(done[other * own : (other + 1) * own]):
                sent.add(other)
                ag[other] = wide[:, other * own : (other + 1) * own]

                @pl.when(b != other)
                def _(other=other):
                    ad_copy(other).start()

    total = ag[b]
    for d in range(1, nb):
        ad_copy(lax.rem(b + d, nb)).wait()
        total = total + adj_recv[d]
    out_ref[...] = total


def products(spectral, kernel_rows, fwd, mix, nb, nc, focal, waves, own):
    group_columns = kernel_rows.shape[1]
    block_rows = kernel_rows.shape[0] // (2 * waves)
    samples = spectral.shape[1]
    rows = 2 * waves * focal
    chunk = next(size for size in (64, 32, 16, 8) if kernel_rows.shape[0] % size == 0)
    lines, tiles, slots = own // LINE, samples // 128, 4
    dma = pltpu.SemaphoreType.DMA
    moved = 4 * (spectral.size + kernel_rows.size)
    return pl.pallas_call(
        functools.partial(kernel, nb, nc, focal, waves, block_rows, group_columns, own, chunk),
        out_shape=jax.ShapeDtypeStruct((rows, own), F32),
        in_specs=[pl.BlockSpec(memory_space=pl.ANY)] * 2 + [pl.BlockSpec(memory_space=pltpu.VMEM)] * 2,
        out_specs=pl.BlockSpec(memory_space=pltpu.VMEM),
        scratch_shapes=[
            pltpu.VMEM((min(lines, 3), tiles, LINE * focal, 128), F32),
            pltpu.VMEM((slots, chunk, group_columns), F32),
            pltpu.VMEM(kernel_rows.shape, BF16),
            pltpu.VMEM(kernel_rows.shape, BF16),
            pltpu.VMEM((lines, rows, LINE), F32),
            pltpu.VMEM((nb, rows, own), F32),
            pltpu.VMEM((rows, block_rows), F32),
            pltpu.VMEM((rows, group_columns), F32),
            pltpu.VMEM((2, group_columns, 2 * rows), BF16),
            pltpu.VMEM((nc, rows, own), F32),
            pltpu.VMEM((nc, rows, own), F32),
            pltpu.VMEM((nc, rows, own), F32),
            pltpu.VMEM((2, 2 * rows, block_rows), BF16),
            pltpu.VMEM((nb, rows, own), F32),
            dma((min(lines, 3), tiles)), dma((slots,)),
            dma((nb,)), dma((nb,)), dma((nc,)), dma((nc,)), dma((nc,)), dma((nc,)), dma((nb,)), dma((nb,)),
        ],
        compiler_params=pltpu.CompilerParams(
            collective_id=0, has_side_effects=True, vmem_limit_bytes=63 << 20
        ),
        cost_estimate=pl.CostEstimate(
            flops=16 * kernel_rows.size * focal, bytes_accessed=moved, transcendentals=0
        ),
    )(spectral, kernel_rows, fwd, mix)


def local(focusing_plus, direct_field, reflectivity, frequency_bins, focal_onsets, line_offsets, nb, nc):
    own, focal, samples = focusing_plus.shape
    waves, _, block_rows, group_columns = reflectivity.shape
    forward, inverse = wave_tables(frequency_bins, samples)
    block_index = lax.axis_index("blk")
    group_index = lax.axis_index("cols")

    first_share = block_index * block_rows + group_index * own
    window = windows(first_share, own, focal_onsets, line_offsets, samples)
    mix = jnp.einsum(
        "flt,kjt->kjfl", window.astype(F32), forward[:, None] * inverse[None],
        precision=highest,
    )
    mix = jnp.repeat(mix, LINE, axis=3).reshape(-1, own)
    fwd = jnp.pad(forward, ((0, 8 - 2 * waves), (0, 0)))
    update = products(
        focusing_plus.reshape(own * focal, samples), reflectivity.reshape(-1, group_columns),
        fwd, mix, nb, nc, focal, waves, own,
    )

    first_source = group_index * group_columns + block_index * own
    window = windows(first_source, own, focal_onsets, line_offsets, samples)
    window = jnp.repeat(window.transpose(1, 0, 2), LINE, axis=0)
    update = update.reshape(2 * waves, focal, own).transpose(0, 2, 1).reshape(2 * waves, -1)
    correction = lax.dot_general(
        update, inverse, (((0,), (0,)), ((), ())),
        precision=high, preferred_element_type=jnp.float32,
    ).reshape(own, focal, samples)
    return direct_field - jnp.where(window, correction, jnp.zeros_like(correction))


def solution(mesh):
    nb, nc = mesh.shape["blk"], mesh.shape["cols"]
    return jax.shard_map(
        functools.partial(local, nb=nb, nc=nc),
        mesh=mesh,
        in_specs=(
            P(("cols", "blk"), None, None),
            P(("cols", "blk"), None, None),
            P(None, None, "blk", "cols"),
            P(),
            P(),
            P(),
        ),
        out_specs=P(("cols", "blk"), None, None),
        check_vma=False,
    )
```

time: 213 us -> 93.2 us (0.44)
  the two profiles are of different devices: /device:TPU:0 before, /device:TPU:19 now
where the time goes in v2:
time: 93.2 us; the launch traced here: 92.5 us
  Pallas kernels  75.9 us (81%)
  matrix products  9.54 us (10%)
  local copies, waits for them, and re-layouts  4.59 us (5%)
  other arithmetic  2.43 us (3%)
    pallas_call x1, Pallas kernels, products(): pl.pallas_call(functools.partial(kernel, nb, nc, focal, waves, block_rows...  75.9 us
    dot_general x1, matrix products, local(): lax.dot_general(update, inverse, (((0,), (0,)), ((), ())), precision=high...  9.1 us

profile of v2, /device:TPU:19, one launch (start us, length us, event | category | flops | bytes accessed | tf_op | source)
XLA Modules:
  0.0 92.5 jit_solution(6659419868568565548)
XLA Ops:
  0.0 0.8 fusion.16
  0.8 0.7 broadcast_add_fusion
  1.5 0.7 broadcast_add_fusion.1
  2.3 0.9 fusion.15
  3.2 0.6 pad.4.fwd_ref
  3.8 0.4 fusion.4
  4.2 0.1 fusion.1
  4.3 0.2 copy.8
  4.5 0.3 broadcast_in_dim.7
  4.9 1.0 %reshape_reshape.3.mix_ref = f32[256,304]{1,0:T(8,128)} reshape(f32[4,4,16,4,76]{4,3,2,1,0:T(4,128)S(1)} %broadcast_in_dim.7) | data formatting | bytes 622592 | tf_op jit(solution)/shard_map/reshape;reshape | solution.py:321
  5.9 75.9 %shard_map.64 = f32[64,304]{1,0:T(8,128)} custom-call(f32[4864,512]{1,0:T(8,128)} %bitcast.19, f32[4864,2432]{1,0:T(8,128)} %bitcast.18, f32[8,512]{1,0:T(8,128)} %pad.4.fwd_ref, f32[256,304]{1,0:T(8,128)} %reshape_reshape.3.mix_ref), custom_call_target="tpu_custom_call" | custom-call | flops 3028287488 | bytes 57278464 | tf_op jit(solution)/shard_map/pallas_call | solution.py:276
  81.8 1.1 %copy.9 = f32[4,16,304]{1,2,0:T(8,128)S(1)} copy(f32[4,16,304]{2,1,0:T(8,128)} %bitcast.21) | data formatting | bytes 155648 | tf_op jit(solution)/shard_map/reshape | solution.py:331
  82.9 0.3 reshape.225
  83.2 0.2 dot_general.12
  83.4 9.1 %select_subtract_fusion = f32[304,16,512]{2,1,0:T(8,128)} fusion(f32[304,16,512]{2,1,0:T(8,128)} %param.7, pred[4,16,512]{2,1,0:T(8,128)(4,1)S(1)} %fusion.1, f32[4,512,1]{1,0,2:T(4,128)S(1)} %reshape.228, f32[304,16,4]{1,0,2:T(8,128)S(1)} %dot_general.12), kind=kOutput, calls=%fused_computation | convolution fusion | flops 64749568 | bytes 20041728 | tf_op jit(solution)/shard_map/dot_general | solution.py:332
  (4 shorter events, 0.0 us)

commit v3 on v2

--- a/solution.py
+++ b/solution.py
@@ -14,24 +14,12 @@
 BF16 = jnp.bfloat16
 
 
-high = lax.Precision.HIGH
-highest = lax.Precision.HIGHEST
-
-
 def wave_tables(frequency_bins, samples):
     times = jnp.arange(samples, dtype=jnp.int32)
     phases = frequency_bins[:, None] * times[None, :] % samples
     angles = phases.astype(jnp.float32) * (2.0 * math.pi / samples)
     inverse = jnp.stack([jnp.cos(angles), -jnp.sin(angles)], axis=1).reshape(-1, samples)
-    forward = inverse / math.sqrt(samples)
-    return (forward, inverse)
-
-
-def windows(first_row, positions, focal_onsets, line_offsets, samples):
-    lines = lax.dynamic_slice_in_dim(line_offsets, first_row // LINE, positions // LINE)
-    onsets = (focal_onsets[:, None] + lines[None, :])[:, :, None]
-    times = jnp.arange(samples, dtype=jnp.int32)
-    return (times < onsets) | (times >= samples - onsets)
+    return inverse
 
 
 def split(value):
@@ -52,8 +40,8 @@
 
 def kernel(
     nb, nc, focal, waves, block_rows, group_columns, own, chunk,
-    x_hbm, k_hbm, fwd_ref, mix_ref, out_ref,
-    xbuf, stage, upper, lower, spec, ag, table, wide, right, up_send, up_recv, mins, left, adj_recv,
+    x_hbm, k_hbm, inv_ref, onset_ref, out_ref,
+    xbuf, stage, upper, lower, spec, mix_ref, ag, table, wide, right, up_send, up_recv, mins, left, adj_recv,
     x_sem, k_sem, ag_s, ag_r, up_s, up_r, mi_s, mi_r, ad_s, ad_r,
 ):
     b = lax.axis_index("blk")
@@ -96,7 +84,7 @@
         pl.semaphore_signal(barrier, inc=1, device_id=to_cols(lax.rem(c + d, nc)), device_id_type=MESH)
     pl.semaphore_wait(barrier, nb + nc - 2)
 
-    fwd = jnp.concatenate(split(fwd_ref[...]), axis=0).astype(BF16)
+    fwd = jnp.concatenate(split(inv_ref[...] / math.sqrt(inv_ref.shape[1])), axis=0).astype(BF16)
     for line in range(lines):
         for tile in range(lane_tiles):
             x_copy(line, tile).wait()
@@ -118,17 +106,26 @@
     for line in range(lines):
         ag[b, :, line * LINE : (line + 1) * LINE] = spec[line]
 
+    partner = b + 1 - 2 * lax.rem(b, 2)
+    pairs = nb // 2
+
     def ag_copy(d):
         return pltpu.make_async_remote_copy(
             src_ref=ag.at[b], dst_ref=ag.at[b], send_sem=ag_s.at[d], recv_sem=ag_r.at[d],
-            device_id=to_blk(lax.rem(b + d, nb)), device_id_type=MESH,
-        )
-
-    for d in range(1, nb):
+            device_id=to_blk(lax.rem(b + 2 * d, nb) if d else partner), device_id_type=MESH,
+        )
+
+    def ag_pass(d):
+        source = lax.rem(b - 2 * d + nb, nb)
+        return pltpu.make_async_remote_copy(
+            src_ref=ag.at[source], dst_ref=ag.at[source], send_sem=ag_s.at[pairs + d], recv_sem=ag_r.at[pairs + d],
+            device_id=to_blk(partner), device_id_type=MESH,
+        )
+
+    for d in list(range(1, pairs)) + [0]:
         ag_copy(d).start()
 
-    @pl.loop(0, chunks)
-    def _(index):
+    def take(index):
         slot = lax.rem(index, slots)
         k_copy(index, slot).wait()
         value = stage[slot]
@@ -141,8 +138,31 @@
         def _():
             k_copy(index + slots, slot).start()
 
-    for d in range(1, nb):
-        ag_copy(d).wait()
+    bounds = [0] + [chunks * (d + 1) // (pairs + 2) for d in range(1, pairs)] + [chunks]
+    for d in range(1, pairs + 1):
+        pl.loop(bounds[d - 1], bounds[d])(take)
+        if d < pairs:
+            ag_copy(d).wait_recv()
+            ag_pass(d).start()
+
+    samples = inv_ref.shape[1]
+    times = lax.broadcasted_iota(jnp.int32, (focal, samples), 1)
+    for line in range(lines):
+        onset = onset_ref[line]
+        window = (times < onset) | (times >= samples - onset)
+        for k in range(2 * waves):
+            for j in range(k, 2 * waves):
+                product = inv_ref[k : k + 1, :] * (inv_ref[j : j + 1, :] / math.sqrt(samples))
+                value = jnp.sum(jnp.where(window, product, 0.0), axis=1, keepdims=True)
+                value = jnp.broadcast_to(value, (focal, LINE))
+                for at in ((k, j), (j, k)) if j > k else ((k, j),):
+                    first = (at[0] * 2 * waves + at[1]) * focal
+                    mix_ref[first : first + focal, line * LINE : (line + 1) * LINE] = value
+
+    ag_copy(0).wait()
+    for d in range(1, pairs):
+        ag_copy(d).wait_send()
+        ag_pass(d).wait()
     for other in range(nb):
         wide[:, other * own : (other + 1) * own] = ag[other]
 
@@ -264,7 +284,7 @@
     out_ref[...] = total
 
 
-def products(spectral, kernel_rows, fwd, mix, nb, nc, focal, waves, own):
+def products(spectral, kernel_rows, inverse, onsets, nb, nc, focal, waves, own):
     group_columns = kernel_rows.shape[1]
     block_rows = kernel_rows.shape[0] // (2 * waves)
     samples = spectral.shape[1]
@@ -284,6 +304,7 @@
             pltpu.VMEM(kernel_rows.shape, BF16),
             pltpu.VMEM(kernel_rows.shape, BF16),
             pltpu.VMEM((lines, rows, LINE), F32),
+            pltpu.VMEM((2 * waves * rows, own), F32),
             pltpu.VMEM((nb, rows, own), F32),
             pltpu.VMEM((rows, block_rows), F32),
             pltpu.VMEM((rows, group_columns), F32),
@@ -302,38 +323,59 @@
         cost_estimate=pl.CostEstimate(
             flops=16 * kernel_rows.size * focal, bytes_accessed=moved, transcendentals=0
         ),
-    )(spectral, kernel_rows, fwd, mix)
+    )(spectral, kernel_rows, inverse, onsets)
+
+
+def final(update_ref, inv_ref, onset_ref, direct_ref, out_ref):
+    focal, samples = onset_ref.shape[1], inv_ref.shape[1]
+    value = update_ref[0]
+    value = jnp.concatenate([value, jnp.zeros((8 - value.shape[0], value.shape[1]), F32)], axis=0)
+    upper, lower = split(value)
+    inv_upper, inv_lower = split(inv_ref[...])
+    lhs = jnp.concatenate([upper, upper, lower, lower], axis=0).T.astype(BF16)
+    rhs = jnp.concatenate([inv_upper, inv_lower, inv_upper, inv_lower], axis=0).astype(BF16)
+    correction = jnp.dot(lhs, rhs, preferred_element_type=F32).reshape(-1, focal, samples)
+    onset = onset_ref[0]
+    times = lax.broadcasted_iota(jnp.int32, (focal, samples), 1)
+    window = (times < onset) | (times >= samples - onset)
+    out_ref[...] = direct_ref[...] - jnp.where(window[None], correction, 0.0)
 
 
 def local(focusing_plus, direct_field, reflectivity, frequency_bins, focal_onsets, line_offsets, nb, nc):
     own, focal, samples = focusing_plus.shape
     waves, _, block_rows, group_columns = reflectivity.shape
-    forward, inverse = wave_tables(frequency_bins, samples)
+    lines = own // LINE
+    inverse = wave_tables(frequency_bins, samples)
+    inverse = jnp.pad(inverse, ((0, 8 - 2 * waves), (0, 0)))
     block_index = lax.axis_index("blk")
     group_index = lax.axis_index("cols")
 
-    first_share = block_index * block_rows + group_index * own
-    window = windows(first_share, own, focal_onsets, line_offsets, samples)
-    mix = jnp.einsum(
-        "flt,kjt->kjfl", window.astype(F32), forward[:, None] * inverse[None],
-        precision=highest,
-    )
-    mix = jnp.repeat(mix, LINE, axis=3).reshape(-1, own)
-    fwd = jnp.pad(forward, ((0, 8 - 2 * waves), (0, 0)))
+    def onsets_from(first):
+        offsets = lax.dynamic_slice_in_dim(line_offsets, first // LINE, lines)
+        return (focal_onsets[None, :] + offsets[:, None])[:, :, None]
+
+    share_onsets = onsets_from(block_index * block_rows + group_index * own)
+    source_onsets = onsets_from(group_index * group_columns + block_index * own)
     update = products(
         focusing_plus.reshape(own * focal, samples), reflectivity.reshape(-1, group_columns),
-        fwd, mix, nb, nc, focal, waves, own,
+        inverse, share_onsets, nb, nc, focal, waves, own,
     )
-
-    first_source = group_index * group_columns + block_index * own
-    window = windows(first_source, own, focal_onsets, line_offsets, samples)
-    window = jnp.repeat(window.transpose(1, 0, 2), LINE, axis=0)
-    update = update.reshape(2 * waves, focal, own).transpose(0, 2, 1).reshape(2 * waves, -1)
-    correction = lax.dot_general(
-        update, inverse, (((0,), (0,)), ((), ())),
-        precision=high, preferred_element_type=jnp.float32,
-    ).reshape(own, focal, samples)
-    return direct_field - jnp.where(window, correction, jnp.zeros_like(correction))
+    update = update.reshape(2 * waves, focal, lines, LINE).transpose(2, 0, 3, 1)
+    update = update.reshape(lines, 2 * waves, LINE * focal)
+    block = pl.BlockSpec((LINE, focal, samples), lambda i: (i, 0, 0))
+    return pl.pallas_call(
+        final,
+        grid=(lines,),
+        out_shape=jax.ShapeDtypeStruct(direct_field.shape, F32),
+        in_specs=[
+            pl.BlockSpec((1, 2 * waves, LINE * focal), lambda i: (i, 0, 0)),
+            pl.BlockSpec(inverse.shape, lambda i: (0, 0)),
+            pl.BlockSpec((1, focal, 1), lambda i: (i, 0, 0)),
+            block,
+        ],
+        out_specs=block,
+        compiler_params=pltpu.CompilerParams(vmem_limit_bytes=48 << 20),
+    )(update, inverse, source_onsets, direct_field)
 
 
 def solution(mesh):

time: 93.2 us -> 90.8 us (0.974)
  matrix products: 9.54 us -> 0 us
  Pallas kernels: 75.9 us -> 84.8 us
  local copies, waits for them, and re-layouts: 4.59 us -> 3.03 us
    dot_general x2 -> x0, matrix products: 9.54 us -> none  [the longest x1 9.1 us: local(): lax.dot_general(update, inverse, (((0,), (0,)), ((), ())), precision=high...]
    pallas_call x0 -> x1, Pallas kernels: none -> 8.84 us  [local(): pl.pallas_call(final, grid=(lines,), out_shape=jax.ShapeDtypeStruct(direc...]
    another operation x1 -> x0, local copies, waits for them, and re-layouts: 1.01 us -> none  [local(): mix = jnp.repeat(mix, LINE, axis=3).reshape(-1, own)]
where the time goes in v3:
time: 90.8 us; the launch traced here: 90.1 us
  Pallas kernels  84.8 us (93%)
  local copies, waits for them, and re-layouts  3.03 us (3%)
  other arithmetic  2.23 us (2%)
    pallas_call x1, Pallas kernels, products(): pl.pallas_call(functools.partial(kernel, nb, nc, focal, waves, block_rows...  75.9 us
    pallas_call x1, Pallas kernels, local(): pl.pallas_call(final, grid=(lines,), out_shape=jax.ShapeDtypeStruct(direc...  8.84 us

profile of v3, /device:TPU:19, one launch (start us, length us, event | category | flops | bytes accessed | tf_op | source)
XLA Modules:
  0.0 90.1 jit_solution(12825509263097363136)
XLA Ops:
  0.0 0.8 fusion.4
  0.8 0.9 fusion.3
  1.7 0.6 pad.4.inv_ref
  2.3 1.3 %broadcast_add_fusion = (s32[4,16,1]{2,1,0:T(8,128)S(1)}, s32[4,16,1]{2,1,0:T(8,128)}) fusion(s32[4]{0:T(128)S(1)} %get-tuple-element.7, s32[16]{0:T(128)} %param.10, s32[4]{0:T(128)S(1)} %get-tuple-element.8), kind=kLoop, calls=%fused_computation.2 | loop fusion | flops 128 | bytes 608 | tf_op jit(solution)/shard_map/add | solution.py:355
  3.7 0.0 copy-start
  3.7 75.9 %shard_map.64 = f32[64,304]{1,0:T(8,128)} custom-call(f32[4864,512]{1,0:T(8,128)} %bitcast.4, f32[4864,2432]{1,0:T(8,128)} %bitcast.3, f32[8,512]{1,0:T(8,128)} %pad.4.inv_ref, s32[4,16,1]{2,1,0:T(8,128)} %get-tuple-element.6.onset_ref), custom_call_target="tpu_custom_call" | custom-call | flops 3028287488 | bytes 57278464 | tf_op jit(solution)/shard_map/pallas_call | solution.py:296
  79.6 1.0 %reshape.196 = f32[4,16,4,76]{3,2,1,0:T(4,128)S(1)} reshape(f32[64,304]{1,0:T(8,128)} %shard_map.64) | data formatting | bytes 155648 | tf_op jit(solution)/shard_map/reshape | solution.py:363
  80.6 0.3 copy.8
  80.9 0.3 reshape.197.update_ref
  81.2 0.0 copy-done
  81.2 8.8 %shard_map.65 = f32[304,16,512]{2,1,0:T(8,128)} custom-call(f32[4,4,1216]{2,1,0:T(4,128)S(1)} %reshape.197.update_ref, f32[8,512]{1,0:T(8,128)S(1)} %copy-done, s32[4,16,1]{2,1,0:T(8,128)S(1)} %get-tuple-element.5.onset_ref, f32[304,16,512]{2,1,0:T(8,128)} %direct_ref.1), custom_call_target="tpu_custom_call" | custom-call | tf_op jit(solution)/shard_map/pallas_call | solution.py:366
  (2 shorter events, 0.0 us)
Async XLA Ops:
  3.7 77.5 %copy-start = (f32[8,512]{1,0:T(8,128)S(1)}, f32[8,512]{1,0:T(8,128)}, u32[]{:S(2)}) copy-start(f32[8,512]{1,0:T(8,128)} %pad.4.inv_ref) | copy-start | bytes 49156
